TPU v7x, 32 devices: a whole 2x2x4 slice. The times are simulated.
32 devices in a mesh: lev: 2 (over x), gx: 4 (over z), gy: 4 (over y, core).
Axes of the slice: x: 2, y: 2, z: 4, core: 2. Of those that a mesh axis runs over, the one named last changes fastest.
Arguments:
- initial_conc: float32 [4, 4, 256, 512], P(None, 'lev', 'gx', 'gy'), may hold values from -6 to 6
- diffusivity: float32 [4, 256, 512], P('lev', 'gx', 'gy'), may hold values from 0.02 to 0.2
- wind_east: float32 [4, 256, 512], P('lev', 'gx', 'gy'), may hold values from -0.4 to 0.4
- wind_north: float32 [4, 256, 512], P('lev', 'gx', 'gy'), may hold values from -0.4 to 0.4
- level_weight: float32 [4, 4], P(None, 'lev'), may hold values from 0.05 to 0.5
- sounding_owner: int32 [8192, 1], P(('gx', 'gy')), may hold values from 0 to 15; in each aligned block of 512 rows (0 to 511, 512 to 1023, ...) at most 64 rows name the same one
- sounding_column: int32 [8192], P(('gx', 'gy')), may hold values from 0 to 8191
- observed: float32 [8192], P(('gx', 'gy')), may hold values from -15 to 15
Outputs:
- forecast: float32 [4, 4, 256, 512], P(None, 'lev', 'gx', 'gy')
- model_column: float32 [8192], P(('gx', 'gy'))
- gradient: float32 [4, 4, 256, 512], P(None, 'lev', 'gx', 'gy')
Inputs may be any that keep to these rules, and one draw needn't show every extreme that they name: `sounding_owner`: among the 512 soundings of one device, at most 64 have the same owner, and this many is reached.
All inputs are finite; a program needn't handle non-finite values.
Results may differ from a plain program's by a relative error of at most 0.00002.
Values sent between devices are 32-bit elements; how exact they have to be, the bound alone decides.
A program may use at most 64 MiB of HBM per device.

v0:
```python
import functools
import jax
import jax.numpy as jnp
from jax import lax
from jax.experimental import pallas as pl
from jax.experimental.pallas import tpu as pltpu
from jax.sharding import PartitionSpec as P

STEPS = 4
H = 2 * STEPS
MESH = pl.DeviceIdType.MESH
SIDES = [(-1, 0), (1, 0), (0, -1), (0, 1), (-1, -1), (-1, 1), (1, -1), (1, 1)]


def pieces(value):
    high = value.astype(jnp.bfloat16).astype(jnp.float32)
    rest = value - high
    middle = rest.astype(jnp.bfloat16).astype(jnp.float32)
    return high, middle, rest - middle


def kernel(
    sizes,
    conc_ref, diff_ref, east_ref, north_ref, weight_ref, owner_ref, column_ref, observed_ref,
    forecast_ref, model_ref, grad_ref,
    ext, other, pack, from_left, from_right, coef, mine, snd, count, part, arrived, values, returned,
    halo_send, halo_recv, snd_send, snd_recv, part_send, part_recv, back_send, back_recv,
):
    n_gx, n_gy, tracers, levels, cx, cy = sizes
    groups = n_gx * n_gy
    fields = tracers * levels
    rows, lanes = cx + 2 * H, 2 * cy
    lev, gx, gy = lax.axis_index("lev"), lax.axis_index("gx"), lax.axis_index("gy")
    me = gx * n_gy + gy

    def group_id(d):
        target = lax.rem(me + d, groups)
        return (lev, target // n_gy, lax.rem(target, n_gy))

    ext[:, 0:H, 0:cy] = jnp.zeros((ext.shape[0], H, cy), jnp.float32)
    ext[:, H + cx : rows, 0:cy] = jnp.zeros((ext.shape[0], H, cy), jnp.float32)
    from_left[...] = jnp.zeros(from_left.shape, jnp.float32)
    from_right[...] = jnp.zeros(from_right.shape, jnp.float32)

    barrier = pltpu.get_barrier_semaphore()

    def greet(d, carry):
        pl.semaphore_signal(barrier, inc=1, device_id=group_id(d), device_id_type=MESH)
        return carry

    lax.fori_loop(1, groups, greet, 0)
    pl.semaphore_signal(barrier, inc=1, device_id=(1 - lev, gx, gy), device_id_type=MESH)

    lane = lax.broadcasted_iota(jnp.int32, (cx, cy), 1)
    per = cy // (2 * H)
    packed = [jnp.zeros((cx, cy), jnp.float32) for _ in range(pack.shape[0])]
    for f in range(ext.shape[0]):
        if f < fields:
            field = conc_ref[f]
        else:
            which, l = divmod(f - fields, levels)
            field = (diff_ref, east_ref, north_ref)[which][l]
        ext[f, H : H + cx, 0:cy] = field
        g, at = divmod(f, per)
        shift = 2 * H * at
        moved = pltpu.roll(field, shift, axis=1) if shift else field
        slot = lax.rem(lane + H, cy) // (2 * H)
        packed[g] = jnp.where(slot == at, moved, packed[g])
    for g in range(pack.shape[0]):
        pack[g] = packed[g]
    owner, column = owner_ref[...], column_ref[...]
    nrow = owner.shape[0]
    mine[0:nrow] = ((owner // n_gy) * cx + column // cy).astype(jnp.float32)
    mine[nrow : 2 * nrow] = (lax.rem(owner, n_gy) * cy + lax.rem(column, cy)).astype(jnp.float32)
    mine[2 * nrow : 3 * nrow] = observed_ref[...]
    snd[me] = mine[...]

    pl.semaphore_wait(barrier, groups)

    def inside(dx, dy):
        x, y = gx + dx, gy + dy
        return (x >= 0) & (x < n_gx) & (y >= 0) & (y < n_gy)

    def halo_copy(k):
        dx, dy = SIDES[k]
        start, length, to = {-1: (0, H, H + cx), 0: (0, cx, H), 1: (cx - H, H, 0)}[dx]
        if dy == 0:
            src = ext.at[:, pl.ds(H + start, length), pl.ds(0, cy)]
            dst = ext.at[:, pl.ds(to, length), pl.ds(0, cy)]
        else:
            src = pack.at[:, pl.ds(start, length), :]
            dst = (from_right if dy < 0 else from_left).at[:, pl.ds(to, length), :]
        return pltpu.make_async_remote_copy(
            src_ref=src, dst_ref=dst, send_sem=halo_send.at[k], recv_sem=halo_recv.at[k],
            device_id=(lev, gx + dx, gy + dy), device_id_type=MESH,
        )

    for k, (dx, dy) in enumerate(SIDES):
        pl.when(inside(dx, dy))(lambda k=k: halo_copy(k).start())

    def snd_copy(d):
        return pltpu.make_async_remote_copy(
            src_ref=mine, dst_ref=snd.at[me], send_sem=snd_send.at[d], recv_sem=snd_recv.at[d],
            device_id=group_id(d), device_id_type=MESH,
        )

    def loop_over(low, high, body):
        def step(i, carry):
            body(i)
            return carry

        lax.fori_loop(low, high, step, 0)

    loop_over(1, groups, lambda d: snd_copy(d).start())

    for k, (dx, dy) in enumerate(SIDES):
        pl.when(inside(-dx, -dy))(lambda k=k: halo_copy(k).wait_recv())

    wide = lax.broadcasted_iota(jnp.int32, (rows, cy), 1)
    for g in range(pack.shape[0]):
        both = jnp.where(lax.rem(wide, 2 * H) < H, from_right[g], from_left[g])
        for at in range(min(per, ext.shape[0] - g * per)):
            shift = 2 * H * at
            moved = pltpu.roll(both, cy - shift, axis=1) if shift else both
            ext[g * per + at, :, cy:lanes] = jnp.where((wide < H) | (wide >= cy - H), moved, 0.0)
    for l in range(levels):
        kappa = ext[fields + l]
        u = 0.5 * ext[fields + levels + l]
        v = 0.5 * ext[fields + 2 * levels + l]
        coef[l, 0] = 1.0 - 4.0 * kappa
        coef[l, 1] = kappa - u
        coef[l, 2] = kappa + u
        coef[l, 3] = kappa - v
        coef[l, 4] = kappa + v

    def stepped(c, l):
        return (
            coef[l, 0] * c
            + coef[l, 1] * pltpu.roll(c, rows - 1, axis=0)
            + coef[l, 2] * pltpu.roll(c, 1, axis=0)
            + coef[l, 3] * pltpu.roll(c, lanes - 1, axis=1)
            + coef[l, 4] * pltpu.roll(c, 1, axis=1)
        )

    for step in range(STEPS):
        source, target = (ext, other) if step % 2 == 0 else (other, ext)
        if step == 1:
            for k, (dx, dy) in enumerate(SIDES):
                pl.when(inside(dx, dy))(lambda k=k: halo_copy(k).wait_send())
        if step < STEPS - 1:
            def advance(t):
                for l in range(levels):
                    target[t * levels + l] = stepped(source[t * levels + l], l)

            loop_over(0, tracers, advance)
        else:
            part[...] = jnp.zeros(part.shape, jnp.float32)

            def finish(t):
                total = part[...]
                for l in range(levels):
                    result = stepped(source[t * levels + l], l)
                    forecast_ref[t * levels + l] = result[H : H + cx, 0:cy]
                    total = total + weight_ref[t, l] * result
                part[...] = total

            loop_over(0, tracers, finish)

    part_copy = pltpu.make_async_remote_copy(
        src_ref=part, dst_ref=arrived, send_sem=part_send, recv_sem=part_recv,
        device_id=(1 - lev, gx, gy), device_id_type=MESH,
    )
    part_copy.start()

    loop_over(1, groups, lambda d: snd_copy(d).wait_recv())
    loop_over(1, groups, lambda d: snd_copy(d).wait_send())
    at_once = 4
    x0 = (gx * cx).astype(jnp.float32)
    y0 = (gy * cy).astype(jnp.float32)

    def row_of(base, kind):
        return jnp.concatenate(
            [snd[base + b, kind * nrow + r : kind * nrow + r + 1, :] for b in range(at_once) for r in range(nrow)],
            axis=1,
        )

    span = at_once * nrow * snd.shape[2]
    compact = cy + 2 * H
    count[...] = jnp.zeros(count.shape, jnp.float32)

    def tally(i):
        base = i * at_once
        xs = row_of(base, 0) - (x0 - H)
        ys = row_of(base, 1) - (y0 - H)
        obs = row_of(base, 2)
        at_x = lax.broadcasted_iota(jnp.int32, (rows, span), 0).astype(jnp.float32) == xs
        at_y = lax.broadcasted_iota(jnp.int32, (compact, span), 0).astype(jnp.float32) == ys
        stack = [jnp.where(at_x, 1.0, 0.0)] + [jnp.where(at_x, piece, 0.0) for piece in pieces(obs)]
        left = jnp.concatenate([s.astype(jnp.bfloat16) for s in stack], axis=0)
        right = jnp.where(at_y, 1.0, 0.0).astype(jnp.bfloat16)
        count[:, 0:compact] += lax.dot_general(
            left, right, (((1,), (1,)), ((), ())), preferred_element_type=jnp.float32
        )

    loop_over(0, groups // at_once, tally)

    part_copy.wait()
    field = part[...] + arrived[...]
    number = pltpu.roll(count[0:rows], lanes - H, axis=1)
    total = pltpu.roll(
        count[rows : 2 * rows] + count[2 * rows : 3 * rows] + count[3 * rows : 4 * rows], lanes - H, axis=1
    )
    forcing = number * field - total

    centre = field[H : H + cx, 0:cy]
    stacked = jnp.concatenate(list(pieces(centre)) + [jnp.zeros_like(centre)], axis=0)
    turned = stacked.T.astype(jnp.bfloat16)

    def look_up(i):
        base = i * at_once
        xs = row_of(base, 0) - x0
        ys = row_of(base, 1) - y0
        at_x = lax.broadcasted_iota(jnp.int32, (cx, span), 0).astype(jnp.float32) == xs
        at_y = lax.broadcasted_iota(jnp.int32, (cy, span), 0).astype(jnp.float32) == ys
        pick = jnp.where(at_x, 1.0, 0.0).astype(jnp.bfloat16)
        picked = jnp.dot(
            turned, jnp.concatenate([pick] * 4, axis=0), preferred_element_type=jnp.float32
        )
        found = jnp.sum(jnp.where(at_y, picked, 0.0), axis=0, keepdims=True)
        width = snd.shape[2]
        for b in range(at_once):
            for r in range(nrow):
                k = b * nrow + r
                values[base + b, r : r + 1, :] = found[:, k * width : (k + 1) * width]

    loop_over(0, groups // at_once, look_up)

    def back_copy(d):
        return pltpu.make_async_remote_copy(
            src_ref=values.at[lax.rem(me + d, groups)], dst_ref=returned.at[d],
            send_sem=back_send.at[d], recv_sem=back_recv.at[d],
            device_id=group_id(d), device_id_type=MESH,
        )

    loop_over(1, groups, lambda d: back_copy(d).start())

    for l in range(levels):
        adj = forcing
        for step in range(STEPS):
            adj = (
                coef[l, 0] * adj
                + pltpu.roll(coef[l, 2] * adj, rows - 1, axis=0)
                + pltpu.roll(coef[l, 1] * adj, 1, axis=0)
                + pltpu.roll(coef[l, 4] * adj, lanes - 1, axis=1)
                + pltpu.roll(coef[l, 3] * adj, 1, axis=1)
            )
        inner = adj[H : H + cx, 0:cy]
        for t in range(tracers):
            grad_ref[t * levels + l] = weight_ref[t, l] * inner

    loop_over(1, groups, lambda d: back_copy(d).wait_recv())
    model = values[me]
    for d in range(1, groups):
        model = model + returned[d]
    model_ref[...] = model
    loop_over(1, groups, lambda d: back_copy(d).wait_send())


def shards(n_gx, n_gy, initial_conc, diffusivity, wind_east, wind_north, level_weight, owner, column, observed):
    tracers, levels, cx, cy = initial_conc.shape
    fields = tracers * levels
    total = fields + 3 * levels
    groups = n_gx * n_gy
    count = column.shape[0]
    width = min(128, count)
    nrow = count // width
    rows, lanes = cx + 2 * H, 2 * cy
    per = cy // (2 * H)
    packs = -(-total // per)
    f32 = jnp.float32
    vmem = pl.BlockSpec(memory_space=pltpu.VMEM)
    dma = pltpu.SemaphoreType.DMA
    conc, model, grad = pl.pallas_call(
        functools.partial(kernel, (n_gx, n_gy, tracers, levels, cx, cy)),
        out_shape=(
            jax.ShapeDtypeStruct((fields, cx, cy), f32),
            jax.ShapeDtypeStruct((nrow, width), f32),
            jax.ShapeDtypeStruct((fields, cx, cy), f32),
        ),
        in_specs=[vmem] * 4 + [pl.BlockSpec(memory_space=pltpu.SMEM)] + [vmem] * 3,
        out_specs=(vmem, vmem, vmem),
        scratch_shapes=[
            pltpu.VMEM((total, rows, lanes), f32),
            pltpu.VMEM((fields, rows, lanes), f32),
            pltpu.VMEM((packs, cx, cy), f32),
            pltpu.VMEM((packs, rows, cy), f32),
            pltpu.VMEM((packs, rows, cy), f32),
            pltpu.VMEM((levels, 5, rows, lanes), f32),
            pltpu.VMEM((3 * nrow, width), f32),
            pltpu.VMEM((groups, 3 * nrow, width), f32),
            pltpu.VMEM((4 * rows, lanes), f32),
            pltpu.VMEM((rows, lanes), f32),
            pltpu.VMEM((rows, lanes), f32),
            pltpu.VMEM((groups, nrow, width), f32),
            pltpu.VMEM((groups, nrow, width), f32),
            dma((len(SIDES),)), dma((len(SIDES),)),
            dma((groups,)), dma((groups,)),
            dma, dma,
            dma((groups,)), dma((groups,)),
        ],
        compiler_params=pltpu.CompilerParams(
            collective_id=0, has_side_effects=True, vmem_limit_bytes=48 * 1024 * 1024
        ),
        cost_estimate=pl.CostEstimate(flops=2 * 10**9, bytes_accessed=2 * 10**6, transcendentals=0),
    )(
        initial_conc.reshape(fields, cx, cy), diffusivity, wind_east, wind_north, level_weight,
        owner.reshape(nrow, width), column.reshape(nrow, width), observed.reshape(nrow, width),
    )
    shape = (tracers, levels, cx, cy)
    return conc.reshape(shape), model.reshape(count), grad.reshape(shape)


def solution(mesh):
    return jax.shard_map(
        functools.partial(shards, mesh.shape["gx"], mesh.shape["gy"]),
        mesh=mesh,
        in_specs=(
            P(None, "lev", "gx", "gy"),
            P("lev", "gx", "gy"),
            P("lev", "gx", "gy"),
            P("lev", "gx", "gy"),
            P(None, "lev"),
            P(("gx", "gy"), None),
            P(("gx", "gy")),
            P(("gx", "gy")),
        ),
        out_specs=(P(None, "lev", "gx", "gy"), P(("gx", "gy")), P(None, "lev", "gx", "gy")),
        check_vma=False,
    )
```

profile of v0, /device:TPU:0, one launch (start us, length us, event | category | flops | bytes accessed | tf_op | source)
XLA Modules:
  0.0 30.1 jit_solution(7454879382118221560)
XLA Ops:
  0.6 0.0 copy-start.7
  0.6 0.0 copy-start.6
  0.7 0.0 copy-start.4
  0.7 0.0 copy-start.5
  0.7 0.6 %copy-done.7 = f32[4,2]{0,1:T(2,128)S(1)} copy-done((f32[4,2]{0,1:T(2,128)S(1)}, f32[4,2]{0,1:T(2,128)}, u32[]{:S(2)}) %copy-start.7) | copy-done | bytes 56
  1.3 0.1 copy.11.weight_ref
  1.4 0.0 copy-done.6
  1.4 0.0 copy-done.4
  1.4 0.0 copy-done.5
  1.4 0.0 copy-start
  1.4 0.9 %copy-done = f32[4,2,64,128]{3,2,1,0:T(8,128)S(1)} copy-done((f32[4,2,64,128]{3,2,1,0:T(8,128)S(1)}, f32[4,2,64,128]{3,2,1,0:T(8,128)}, u32[]{:S(2)}) %copy-start) | copy-done | bytes 262168
  2.4 0.0 copy-start.1
  2.4 0.8 %copy-done.1 = f32[2,64,128]{2,1,0:T(8,128)S(1)} copy-done((f32[2,64,128]{2,1,0:T(8,128)S(1)}, f32[2,64,128]{2,1,0:T(8,128)}, u32[]{:S(2)}) %copy-start.1) | copy-done | bytes 65560
  3.2 0.0 copy-start.2
  3.2 0.8 %copy-done.2 = f32[2,64,128]{2,1,0:T(8,128)S(1)} copy-done((f32[2,64,128]{2,1,0:T(8,128)S(1)}, f32[2,64,128]{2,1,0:T(8,128)}, u32[]{:S(2)}) %copy-start.2) | copy-done | bytes 65560
  4.0 0.0 copy-start.3
  4.0 0.8 %copy-done.3 = f32[2,64,128]{2,1,0:T(8,128)S(1)} copy-done((f32[2,64,128]{2,1,0:T(8,128)S(1)}, f32[2,64,128]{2,1,0:T(8,128)}, u32[]{:S(2)}) %copy-start.3) | copy-done | bytes 65560
  4.9 23.2 %shard_map.103 = (f32[8,64,128]{2,1,0:T(8,128)S(1)}, f32[4,128]{1,0:T(4,128)S(1)}, f32[8,64,128]{2,1,0:T(8,128)S(1)}) custom-call(f32[8,64,128]{2,1,0:T(8,128)S(1)} %bitcast.10, f32[2,64,128]{2,1,0:T(8,128)S(1)} %copy-done.1, f32[2,64,128]{2,1,0:T(8,128)S(1)} %copy-done.2, f32[2,64,128]{2,1,0:T(8,128)S(1)} %copy-done.3, f32[4,2]{1,0:T(4,128)S(1)} %copy.11.weight_ref, ...), custom_call_target="tpu_custom_call" | custom-call | flops 2000000000 | bytes 2000000 | tf_op jit(solution)/shard_map/pallas_call | solution.py:283
  28.1 0.7 %copy.15 = f32[4,2,64,128]{3,2,1,0:T(8,128)} copy(f32[4,2,64,128]{3,2,1,0:T(8,128)S(1)} %bitcast.8) | data formatting | bytes 524288
  28.8 0.6 %copy.16 = f32[512]{0:T(512)} copy(f32[512]{0:T(512)S(1)} %bitcast.9) | data formatting | bytes 4096
  29.4 0.7 %copy.17 = f32[4,2,64,128]{3,2,1,0:T(8,128)} copy(f32[4,2,64,128]{3,2,1,0:T(8,128)S(1)} %bitcast.7) | data formatting | bytes 524288
Async XLA Ops:
  0.6 0.7 %copy-start.7 = (f32[4,2]{0,1:T(2,128)S(1)}, f32[4,2]{0,1:T(2,128)}, u32[]{:S(2)}) copy-start(f32[4,2]{0,1:T(2,128)} %param.12) | copy-start | bytes 100
  0.6 0.8 %copy-start.6 = (f32[512]{0:T(512)S(1)}, f32[512]{0:T(512)}, u32[]{:S(2)}) copy-start(f32[512]{0:T(512)} %param.15) | copy-start | bytes 6148
  0.7 0.8 %copy-start.4 = (s32[512,1]{0,1:T(1,128)S(1)}, s32[512,1]{0,1:T(1,128)}, u32[]{:S(2)}) copy-start(s32[512,1]{0,1:T(1,128)} %param.13) | copy-start | bytes 6148
  0.7 0.8 %copy-start.5 = (s32[512]{0:T(512)S(1)}, s32[512]{0:T(512)}, u32[]{:S(2)}) copy-start(s32[512]{0:T(512)} %param.14) | copy-start | bytes 6148
  1.4 1.0 %copy-start = (f32[4,2,64,128]{3,2,1,0:T(8,128)S(1)}, f32[4,2,64,128]{3,2,1,0:T(8,128)}, u32[]{:S(2)}) copy-start(f32[4,2,64,128]{3,2,1,0:T(8,128)} %param.8) | copy-start | bytes 786436
  2.4 0.8 %copy-start.1 = (f32[2,64,128]{2,1,0:T(8,128)S(1)}, f32[2,64,128]{2,1,0:T(8,128)}, u32[]{:S(2)}) copy-start(f32[2,64,128]{2,1,0:T(8,128)} %diff_ref.1) | copy-start | bytes 196612
  3.2 0.8 %copy-start.2 = (f32[2,64,128]{2,1,0:T(8,128)S(1)}, f32[2,64,128]{2,1,0:T(8,128)}, u32[]{:S(2)}) copy-start(f32[2,64,128]{2,1,0:T(8,128)} %east_ref.1) | copy-start | bytes 196612
  4.0 0.8 %copy-start.3 = (f32[2,64,128]{2,1,0:T(8,128)S(1)}, f32[2,64,128]{2,1,0:T(8,128)}, u32[]{:S(2)}) copy-start(f32[2,64,128]{2,1,0:T(8,128)} %north_ref.1) | copy-start | bytes 196612
where the time goes:
time: 30.4 us; the launch traced here: 30.1 us
  Pallas kernels  23.2 us (76%)
  local copies, waits for them, and re-layouts  6.19 us (20%)
  between operations  0.69 us (2%)
    pallas_call x1, Pallas kernels, shards(): pl.pallas_call(functools.partial(kernel, (n_gx, n_gy, tracers, levels, cx...  23.2 us
    unnamed x20, local copies, waits for them, and re-layouts  6.19 us

commit v1 on v0

--- a/solution.py
+++ b/solution.py
@@ -25,6 +25,7 @@
     forecast_ref, model_ref, grad_ref,
     ext, other, pack, from_left, from_right, coef, mine, snd, count, part, arrived, values, returned,
     halo_send, halo_recv, snd_send, snd_recv, part_send, part_recv, back_send, back_recv,
+    owner_in, column_in, observed_in, load_sem,
 ):
     n_gx, n_gy, tracers, levels, cx, cy = sizes
     groups = n_gx * n_gy
@@ -37,6 +38,17 @@
         target = lax.rem(me + d, groups)
         return (lev, target // n_gy, lax.rem(target, n_gy))
 
+    loads = []
+    begin = 0
+    for ref in (conc_ref, diff_ref, east_ref, north_ref):
+        place = ext.at[pl.ds(begin, ref.shape[0]), pl.ds(H, cx), pl.ds(0, cy)]
+        loads.append(pltpu.make_async_copy(ref, place, load_sem.at[len(loads)]))
+        begin += ref.shape[0]
+    for ref, place in ((owner_ref, owner_in), (column_ref, column_in), (observed_ref, observed_in)):
+        loads.append(pltpu.make_async_copy(ref, place, load_sem.at[len(loads)]))
+    for load in loads:
+        load.start()
+
     ext[:, 0:H, 0:cy] = jnp.zeros((ext.shape[0], H, cy), jnp.float32)
     ext[:, H + cx : rows, 0:cy] = jnp.zeros((ext.shape[0], H, cy), jnp.float32)
     from_left[...] = jnp.zeros(from_left.shape, jnp.float32)
@@ -51,16 +63,14 @@
     lax.fori_loop(1, groups, greet, 0)
     pl.semaphore_signal(barrier, inc=1, device_id=(1 - lev, gx, gy), device_id_type=MESH)
 
+    for load in loads:
+        load.wait()
+
     lane = lax.broadcasted_iota(jnp.int32, (cx, cy), 1)
     per = cy // (2 * H)
     packed = [jnp.zeros((cx, cy), jnp.float32) for _ in range(pack.shape[0])]
     for f in range(ext.shape[0]):
-        if f < fields:
-            field = conc_ref[f]
-        else:
-            which, l = divmod(f - fields, levels)
-            field = (diff_ref, east_ref, north_ref)[which][l]
-        ext[f, H : H + cx, 0:cy] = field
+        field = ext[f, H : H + cx, 0:cy]
         g, at = divmod(f, per)
         shift = 2 * H * at
         moved = pltpu.roll(field, shift, axis=1) if shift else field
@@ -68,11 +78,11 @@
         packed[g] = jnp.where(slot == at, moved, packed[g])
     for g in range(pack.shape[0]):
         pack[g] = packed[g]
-    owner, column = owner_ref[...], column_ref[...]
+    owner, column = owner_in[...], column_in[...]
     nrow = owner.shape[0]
     mine[0:nrow] = ((owner // n_gy) * cx + column // cy).astype(jnp.float32)
     mine[nrow : 2 * nrow] = (lax.rem(owner, n_gy) * cy + lax.rem(column, cy)).astype(jnp.float32)
-    mine[2 * nrow : 3 * nrow] = observed_ref[...]
+    mine[2 * nrow : 3 * nrow] = observed_in[...]
     snd[me] = mine[...]
 
     pl.semaphore_wait(barrier, groups)
@@ -279,6 +289,7 @@
     packs = -(-total // per)
     f32 = jnp.float32
     vmem = pl.BlockSpec(memory_space=pltpu.VMEM)
+    held = pl.BlockSpec(memory_space=pl.ANY)
     dma = pltpu.SemaphoreType.DMA
     conc, model, grad = pl.pallas_call(
         functools.partial(kernel, (n_gx, n_gy, tracers, levels, cx, cy)),
@@ -287,7 +298,7 @@
             jax.ShapeDtypeStruct((nrow, width), f32),
             jax.ShapeDtypeStruct((fields, cx, cy), f32),
         ),
-        in_specs=[vmem] * 4 + [pl.BlockSpec(memory_space=pltpu.SMEM)] + [vmem] * 3,
+        in_specs=[held] * 4 + [pl.BlockSpec(memory_space=pltpu.SMEM)] + [held] * 3,
         out_specs=(vmem, vmem, vmem),
         scratch_shapes=[
             pltpu.VMEM((total, rows, lanes), f32),
@@ -307,6 +318,10 @@
             dma((groups,)), dma((groups,)),
             dma, dma,
             dma((groups,)), dma((groups,)),
+            pltpu.VMEM((nrow, width), jnp.int32),
+            pltpu.VMEM((nrow, width), jnp.int32),
+            pltpu.VMEM((nrow, width), f32),
+            dma((7,)),
         ],
         compiler_params=pltpu.CompilerParams(
             collective_id=0, has_side_effects=True, vmem_limit_bytes=48 * 1024 * 1024

time: 30.4 us -> 30.5 us (level)
  no operation moved by 1% of the time
where the time goes in v1:
time: 30.5 us; the launch traced here: 30.2 us
  Pallas kernels  23.3 us (76%)
  local copies, waits for them, and re-layouts  6.19 us (20%)
  between operations  0.69 us (2%)
    pallas_call x1, Pallas kernels, shards(): pl.pallas_call(functools.partial(kernel, (n_gx, n_gy, tracers, levels, cx...  23.3 us
    unnamed x20, local copies, waits for them, and re-layouts  6.19 us

profile of v1, /device:TPU:0, one launch (start us, length us, event | category | flops | bytes accessed | tf_op | source)
XLA Modules:
  0.0 30.2 jit_solution(15304410978599411028)
XLA Ops:
  0.6 0.0 copy-start.7
  0.6 0.0 copy-start.6
  0.7 0.0 copy-start.4
  0.7 0.0 copy-start.5
  0.7 0.6 %copy-done.7 = f32[4,2]{0,1:T(2,128)S(1)} copy-done((f32[4,2]{0,1:T(2,128)S(1)}, f32[4,2]{0,1:T(2,128)}, u32[]{:S(2)}) %copy-start.7) | copy-done | bytes 56
  1.3 0.1 copy.11.weight_ref
  1.4 0.0 copy-done.6
  1.4 0.0 copy-done.4
  1.4 0.0 copy-done.5
  1.4 0.0 copy-start
  1.4 0.9 %copy-done = f32[4,2,64,128]{3,2,1,0:T(8,128)S(1)} copy-done((f32[4,2,64,128]{3,2,1,0:T(8,128)S(1)}, f32[4,2,64,128]{3,2,1,0:T(8,128)}, u32[]{:S(2)}) %copy-start) | copy-done | bytes 262168
  2.4 0.0 copy-start.1
  2.4 0.8 %copy-done.1 = f32[2,64,128]{2,1,0:T(8,128)S(1)} copy-done((f32[2,64,128]{2,1,0:T(8,128)S(1)}, f32[2,64,128]{2,1,0:T(8,128)}, u32[]{:S(2)}) %copy-start.1) | copy-done | bytes 65560
  3.2 0.0 copy-start.2
  3.2 0.8 %copy-done.2 = f32[2,64,128]{2,1,0:T(8,128)S(1)} copy-done((f32[2,64,128]{2,1,0:T(8,128)S(1)}, f32[2,64,128]{2,1,0:T(8,128)}, u32[]{:S(2)}) %copy-start.2) | copy-done | bytes 65560
  4.0 0.0 copy-start.3
  4.0 0.8 %copy-done.3 = f32[2,64,128]{2,1,0:T(8,128)S(1)} copy-done((f32[2,64,128]{2,1,0:T(8,128)S(1)}, f32[2,64,128]{2,1,0:T(8,128)}, u32[]{:S(2)}) %copy-start.3) | copy-done | bytes 65560
  4.9 23.3 %shard_map.103 = (f32[8,64,128]{2,1,0:T(8,128)S(1)}, f32[4,128]{1,0:T(4,128)S(1)}, f32[8,64,128]{2,1,0:T(8,128)S(1)}) custom-call(f32[8,64,128]{2,1,0:T(8,128)S(1)} %bitcast.10, f32[2,64,128]{2,1,0:T(8,128)S(1)} %copy-done.1, f32[2,64,128]{2,1,0:T(8,128)S(1)} %copy-done.2, f32[2,64,128]{2,1,0:T(8,128)S(1)} %copy-done.3, f32[4,2]{1,0:T(4,128)S(1)} %copy.11.weight_ref, ...), custom_call_target="tpu_custom_call" | custom-call | flops 2000000000 | bytes 2000000 | tf_op jit(solution)/shard_map/pallas_call | solution.py:294
  28.2 0.7 %copy.15 = f32[4,2,64,128]{3,2,1,0:T(8,128)} copy(f32[4,2,64,128]{3,2,1,0:T(8,128)S(1)} %bitcast.8) | data formatting | bytes 524288
  28.9 0.6 %copy.16 = f32[512]{0:T(512)} copy(f32[512]{0:T(512)S(1)} %bitcast.9) | data formatting | bytes 4096
  29.5 0.7 %copy.17 = f32[4,2,64,128]{3,2,1,0:T(8,128)} copy(f32[4,2,64,128]{3,2,1,0:T(8,128)S(1)} %bitcast.7) | data formatting | bytes 524288
Async XLA Ops:
  0.6 0.7 %copy-start.7 = (f32[4,2]{0,1:T(2,128)S(1)}, f32[4,2]{0,1:T(2,128)}, u32[]{:S(2)}) copy-start(f32[4,2]{0,1:T(2,128)} %param.12) | copy-start | bytes 100
  0.6 0.8 %copy-start.6 = (f32[512]{0:T(512)S(1)}, f32[512]{0:T(512)}, u32[]{:S(2)}) copy-start(f32[512]{0:T(512)} %param.15) | copy-start | bytes 6148
  0.7 0.8 %copy-start.4 = (s32[512,1]{0,1:T(1,128)S(1)}, s32[512,1]{0,1:T(1,128)}, u32[]{:S(2)}) copy-start(s32[512,1]{0,1:T(1,128)} %param.13) | copy-start | bytes 6148
  0.7 0.8 %copy-start.5 = (s32[512]{0:T(512)S(1)}, s32[512]{0:T(512)}, u32[]{:S(2)}) copy-start(s32[512]{0:T(512)} %param.14) | copy-start | bytes 6148
  1.4 1.0 %copy-start = (f32[4,2,64,128]{3,2,1,0:T(8,128)S(1)}, f32[4,2,64,128]{3,2,1,0:T(8,128)}, u32[]{:S(2)}) copy-start(f32[4,2,64,128]{3,2,1,0:T(8,128)} %param.8) | copy-start | bytes 786436
  2.4 0.8 %copy-start.1 = (f32[2,64,128]{2,1,0:T(8,128)S(1)}, f32[2,64,128]{2,1,0:T(8,128)}, u32[]{:S(2)}) copy-start(f32[2,64,128]{2,1,0:T(8,128)} %diff_ref.1) | copy-start | bytes 196612
  3.2 0.8 %copy-start.2 = (f32[2,64,128]{2,1,0:T(8,128)S(1)}, f32[2,64,128]{2,1,0:T(8,128)}, u32[]{:S(2)}) copy-start(f32[2,64,128]{2,1,0:T(8,128)} %east_ref.1) | copy-start | bytes 196612
  4.0 0.8 %copy-start.3 = (f32[2,64,128]{2,1,0:T(8,128)S(1)}, f32[2,64,128]{2,1,0:T(8,128)}, u32[]{:S(2)}) copy-start(f32[2,64,128]{2,1,0:T(8,128)} %north_ref.1) | copy-start | bytes 196612

commit v2 on v1

--- a/solution.py
+++ b/solution.py
@@ -289,7 +289,7 @@
     packs = -(-total // per)
     f32 = jnp.float32
     vmem = pl.BlockSpec(memory_space=pltpu.VMEM)
-    held = pl.BlockSpec(memory_space=pl.ANY)
+    held = pl.BlockSpec(memory_space=pltpu.HBM)
     dma = pltpu.SemaphoreType.DMA
     conc, model, grad = pl.pallas_call(
         functools.partial(kernel, (n_gx, n_gy, tracers, levels, cx, cy)),

time: 30.5 us -> 30.5 us (level)
  no operation moved by 1% of the time
where the time goes in v2:
time: 30.5 us; the launch traced here: 30.2 us
  Pallas kernels  23.3 us (76%)
  local copies, waits for them, and re-layouts  6.19 us (20%)
  between operations  0.69 us (2%)
    pallas_call x1, Pallas kernels, shards(): pl.pallas_call(functools.partial(kernel, (n_gx, n_gy, tracers, levels, cx...  23.3 us
    unnamed x20, local copies, waits for them, and re-layouts  6.19 us

profile of v2, /device:TPU:0, one launch (start us, length us, event | category | flops | bytes accessed | tf_op | source)
XLA Modules:
  0.0 30.2 jit_solution(15304410978599411028)
XLA Ops:
  0.6 0.0 copy-start.7
  0.6 0.0 copy-start.6
  0.7 0.0 copy-start.4
  0.7 0.0 copy-start.5
  0.7 0.6 %copy-done.7 = f32[4,2]{0,1:T(2,128)S(1)} copy-done((f32[4,2]{0,1:T(2,128)S(1)}, f32[4,2]{0,1:T(2,128)}, u32[]{:S(2)}) %copy-start.7) | copy-done | bytes 56
  1.3 0.1 copy.11.weight_ref
  1.4 0.0 copy-done.6
  1.4 0.0 copy-done.4
  1.4 0.0 copy-done.5
  1.4 0.0 copy-start
  1.4 0.9 %copy-done = f32[4,2,64,128]{3,2,1,0:T(8,128)S(1)} copy-done((f32[4,2,64,128]{3,2,1,0:T(8,128)S(1)}, f32[4,2,64,128]{3,2,1,0:T(8,128)}, u32[]{:S(2)}) %copy-start) | copy-done | bytes 262168
  2.4 0.0 copy-start.1
  2.4 0.8 %copy-done.1 = f32[2,64,128]{2,1,0:T(8,128)S(1)} copy-done((f32[2,64,128]{2,1,0:T(8,128)S(1)}, f32[2,64,128]{2,1,0:T(8,128)}, u32[]{:S(2)}) %copy-start.1) | copy-done | bytes 65560
  3.2 0.0 copy-start.2
  3.2 0.8 %copy-done.2 = f32[2,64,128]{2,1,0:T(8,128)S(1)} copy-done((f32[2,64,128]{2,1,0:T(8,128)S(1)}, f32[2,64,128]{2,1,0:T(8,128)}, u32[]{:S(2)}) %copy-start.2) | copy-done | bytes 65560
  4.0 0.0 copy-start.3
  4.0 0.8 %copy-done.3 = f32[2,64,128]{2,1,0:T(8,128)S(1)} copy-done((f32[2,64,128]{2,1,0:T(8,128)S(1)}, f32[2,64,128]{2,1,0:T(8,128)}, u32[]{:S(2)}) %copy-start.3) | copy-done | bytes 65560
  4.9 23.3 %shard_map.103 = (f32[8,64,128]{2,1,0:T(8,128)S(1)}, f32[4,128]{1,0:T(4,128)S(1)}, f32[8,64,128]{2,1,0:T(8,128)S(1)}) custom-call(f32[8,64,128]{2,1,0:T(8,128)S(1)} %bitcast.10, f32[2,64,128]{2,1,0:T(8,128)S(1)} %copy-done.1, f32[2,64,128]{2,1,0:T(8,128)S(1)} %copy-done.2, f32[2,64,128]{2,1,0:T(8,128)S(1)} %copy-done.3, f32[4,2]{1,0:T(4,128)S(1)} %copy.11.weight_ref, ...), custom_call_target="tpu_custom_call" | custom-call | flops 2000000000 | bytes 2000000 | tf_op jit(solution)/shard_map/pallas_call | solution.py:294
  28.2 0.7 %copy.15 = f32[4,2,64,128]{3,2,1,0:T(8,128)} copy(f32[4,2,64,128]{3,2,1,0:T(8,128)S(1)} %bitcast.8) | data formatting | bytes 524288
  28.9 0.6 %copy.16 = f32[512]{0:T(512)} copy(f32[512]{0:T(512)S(1)} %bitcast.9) | data formatting | bytes 4096
  29.5 0.7 %copy.17 = f32[4,2,64,128]{3,2,1,0:T(8,128)} copy(f32[4,2,64,128]{3,2,1,0:T(8,128)S(1)} %bitcast.7) | data formatting | bytes 524288
Async XLA Ops:
  0.6 0.7 %copy-start.7 = (f32[4,2]{0,1:T(2,128)S(1)}, f32[4,2]{0,1:T(2,128)}, u32[]{:S(2)}) copy-start(f32[4,2]{0,1:T(2,128)} %param.12) | copy-start | bytes 100
  0.6 0.8 %copy-start.6 = (f32[512]{0:T(512)S(1)}, f32[512]{0:T(512)}, u32[]{:S(2)}) copy-start(f32[512]{0:T(512)} %param.15) | copy-start | bytes 6148
  0.7 0.8 %copy-start.4 = (s32[512,1]{0,1:T(1,128)S(1)}, s32[512,1]{0,1:T(1,128)}, u32[]{:S(2)}) copy-start(s32[512,1]{0,1:T(1,128)} %param.13) | copy-start | bytes 6148
  0.7 0.8 %copy-start.5 = (s32[512]{0:T(512)S(1)}, s32[512]{0:T(512)}, u32[]{:S(2)}) copy-start(s32[512]{0:T(512)} %param.14) | copy-start | bytes 6148
  1.4 1.0 %copy-start = (f32[4,2,64,128]{3,2,1,0:T(8,128)S(1)}, f32[4,2,64,128]{3,2,1,0:T(8,128)}, u32[]{:S(2)}) copy-start(f32[4,2,64,128]{3,2,1,0:T(8,128)} %param.8) | copy-start | bytes 786436
  2.4 0.8 %copy-start.1 = (f32[2,64,128]{2,1,0:T(8,128)S(1)}, f32[2,64,128]{2,1,0:T(8,128)}, u32[]{:S(2)}) copy-start(f32[2,64,128]{2,1,0:T(8,128)} %diff_ref.1) | copy-start | bytes 196612
  3.2 0.8 %copy-start.2 = (f32[2,64,128]{2,1,0:T(8,128)S(1)}, f32[2,64,128]{2,1,0:T(8,128)}, u32[]{:S(2)}) copy-start(f32[2,64,128]{2,1,0:T(8,128)} %east_ref.1) | copy-start | bytes 196612
  4.0 0.8 %copy-start.3 = (f32[2,64,128]{2,1,0:T(8,128)S(1)}, f32[2,64,128]{2,1,0:T(8,128)}, u32[]{:S(2)}) copy-start(f32[2,64,128]{2,1,0:T(8,128)} %north_ref.1) | copy-start | bytes 196612

commit v3 on v0

--- a/solution.py
+++ b/solution.py
@@ -152,7 +152,7 @@
                 for l in range(levels):
                     target[t * levels + l] = stepped(source[t * levels + l], l)
 
-            loop_over(0, tracers, advance)
+            lax.fori_loop(0, tracers, lambda t, c: (advance(t), c)[1], 0, unroll=True)
         else:
             part[...] = jnp.zeros(part.shape, jnp.float32)
 
@@ -164,7 +164,7 @@
                     total = total + weight_ref[t, l] * result
                 part[...] = total
 
-            loop_over(0, tracers, finish)
+            lax.fori_loop(0, tracers, lambda t, c: (finish(t), c)[1], 0, unroll=True)
 
     part_copy = pltpu.make_async_remote_copy(
         src_ref=part, dst_ref=arrived, send_sem=part_send, recv_sem=part_recv,

time: 30.4 us -> 29.2 us (0.961)
  Pallas kernels: 23.2 us -> 22 us
    pallas_call x1, Pallas kernels: 23.2 us -> 22 us  [shards(): pl.pallas_call(functools.partial(kernel, (n_gx, n_gy, tracers, levels, cx...]
where the time goes in v3:
time: 29.2 us; the launch traced here: 28.9 us
  Pallas kernels  22 us (75%)
  local copies, waits for them, and re-layouts  6.19 us (21%)
  between operations  0.69 us (2%)
    pallas_call x1, Pallas kernels, shards(): pl.pallas_call(functools.partial(kernel, (n_gx, n_gy, tracers, levels, cx...  22 us
    unnamed x20, local copies, waits for them, and re-layouts  6.19 us

profile of v3, /device:TPU:0, one launch (start us, length us, event | category | flops | bytes accessed | tf_op | source)
XLA Modules:
  0.0 28.9 jit_solution(3002521474934084175)
XLA Ops:
  0.6 0.0 copy-start.7
  0.6 0.0 copy-start.6
  0.7 0.0 copy-start.4
  0.7 0.0 copy-start.5
  0.7 0.6 %copy-done.7 = f32[4,2]{0,1:T(2,128)S(1)} copy-done((f32[4,2]{0,1:T(2,128)S(1)}, f32[4,2]{0,1:T(2,128)}, u32[]{:S(2)}) %copy-start.7) | copy-done | bytes 56
  1.3 0.1 copy.11.weight_ref
  1.4 0.0 copy-done.6
  1.4 0.0 copy-done.4
  1.4 0.0 copy-done.5
  1.4 0.0 copy-start
  1.4 0.9 %copy-done = f32[4,2,64,128]{3,2,1,0:T(8,128)S(1)} copy-done((f32[4,2,64,128]{3,2,1,0:T(8,128)S(1)}, f32[4,2,64,128]{3,2,1,0:T(8,128)}, u32[]{:S(2)}) %copy-start) | copy-done | bytes 262168
  2.4 0.0 copy-start.1
  2.4 0.8 %copy-done.1 = f32[2,64,128]{2,1,0:T(8,128)S(1)} copy-done((f32[2,64,128]{2,1,0:T(8,128)S(1)}, f32[2,64,128]{2,1,0:T(8,128)}, u32[]{:S(2)}) %copy-start.1) | copy-done | bytes 65560
  3.2 0.0 copy-start.2
  3.2 0.8 %copy-done.2 = f32[2,64,128]{2,1,0:T(8,128)S(1)} copy-done((f32[2,64,128]{2,1,0:T(8,128)S(1)}, f32[2,64,128]{2,1,0:T(8,128)}, u32[]{:S(2)}) %copy-start.2) | copy-done | bytes 65560
  4.0 0.0 copy-start.3
  4.0 0.8 %copy-done.3 = f32[2,64,128]{2,1,0:T(8,128)S(1)} copy-done((f32[2,64,128]{2,1,0:T(8,128)S(1)}, f32[2,64,128]{2,1,0:T(8,128)}, u32[]{:S(2)}) %copy-start.3) | copy-done | bytes 65560
  4.9 22.0 %shard_map.103 = (f32[8,64,128]{2,1,0:T(8,128)S(1)}, f32[4,128]{1,0:T(4,128)S(1)}, f32[8,64,128]{2,1,0:T(8,128)S(1)}) custom-call(f32[8,64,128]{2,1,0:T(8,128)S(1)} %bitcast.10, f32[2,64,128]{2,1,0:T(8,128)S(1)} %copy-done.1, f32[2,64,128]{2,1,0:T(8,128)S(1)} %copy-done.2, f32[2,64,128]{2,1,0:T(8,128)S(1)} %copy-done.3, f32[4,2]{1,0:T(4,128)S(1)} %copy.11.weight_ref, ...), custom_call_target="tpu_custom_call" | custom-call | flops 2000000000 | bytes 2000000 | tf_op jit(solution)/shard_map/pallas_call | solution.py:283
  26.9 0.7 %copy.15 = f32[4,2,64,128]{3,2,1,0:T(8,128)} copy(f32[4,2,64,128]{3,2,1,0:T(8,128)S(1)} %bitcast.8) | data formatting | bytes 524288
  27.6 0.6 %copy.16 = f32[512]{0:T(512)} copy(f32[512]{0:T(512)S(1)} %bitcast.9) | data formatting | bytes 4096
  28.2 0.7 %copy.17 = f32[4,2,64,128]{3,2,1,0:T(8,128)} copy(f32[4,2,64,128]{3,2,1,0:T(8,128)S(1)} %bitcast.7) | data formatting | bytes 524288
Async XLA Ops:
  0.6 0.7 %copy-start.7 = (f32[4,2]{0,1:T(2,128)S(1)}, f32[4,2]{0,1:T(2,128)}, u32[]{:S(2)}) copy-start(f32[4,2]{0,1:T(2,128)} %param.12) | copy-start | bytes 100
  0.6 0.8 %copy-start.6 = (f32[512]{0:T(512)S(1)}, f32[512]{0:T(512)}, u32[]{:S(2)}) copy-start(f32[512]{0:T(512)} %param.15) | copy-start | bytes 6148
  0.7 0.8 %copy-start.4 = (s32[512,1]{0,1:T(1,128)S(1)}, s32[512,1]{0,1:T(1,128)}, u32[]{:S(2)}) copy-start(s32[512,1]{0,1:T(1,128)} %param.13) | copy-start | bytes 6148
  0.7 0.8 %copy-start.5 = (s32[512]{0:T(512)S(1)}, s32[512]{0:T(512)}, u32[]{:S(2)}) copy-start(s32[512]{0:T(512)} %param.14) | copy-start | bytes 6148
  1.4 1.0 %copy-start = (f32[4,2,64,128]{3,2,1,0:T(8,128)S(1)}, f32[4,2,64,128]{3,2,1,0:T(8,128)}, u32[]{:S(2)}) copy-start(f32[4,2,64,128]{3,2,1,0:T(8,128)} %param.8) | copy-start | bytes 786436
  2.4 0.8 %copy-start.1 = (f32[2,64,128]{2,1,0:T(8,128)S(1)}, f32[2,64,128]{2,1,0:T(8,128)}, u32[]{:S(2)}) copy-start(f32[2,64,128]{2,1,0:T(8,128)} %diff_ref.1) | copy-start | bytes 196612
  3.2 0.8 %copy-start.2 = (f32[2,64,128]{2,1,0:T(8,128)S(1)}, f32[2,64,128]{2,1,0:T(8,128)}, u32[]{:S(2)}) copy-start(f32[2,64,128]{2,1,0:T(8,128)} %east_ref.1) | copy-start | bytes 196612
  4.0 0.8 %copy-start.3 = (f32[2,64,128]{2,1,0:T(8,128)S(1)}, f32[2,64,128]{2,1,0:T(8,128)}, u32[]{:S(2)}) copy-start(f32[2,64,128]{2,1,0:T(8,128)} %north_ref.1) | copy-start | bytes 196612
